TPU v7x, 32 devices: a whole 2x2x4 slice. The times are simulated.
32 devices in a mesh: gx: 4 (over z), gy: 4 (over x, core), gz: 2 (over y).
Axes of the slice: x: 2, y: 2, z: 4, core: 2. Of those that a mesh axis runs over, the one named last changes fastest.
Arguments:
- gas: float32 [6, 32, 32, 256], P(None, 'gx', 'gy', 'gz'), may hold values from -1.5 to 6, as said below
- parcels: float32 [2048, 5, 128], P(('gx', 'gy', 'gz')), may hold values from -1 to 2, as said below
- home_cell_index: int32 [2048, 128], P(('gx', 'gy', 'gz')), may hold values from 0 to 8191
- order: int32 [32, 64], P(('gx', 'gy', 'gz')), may hold values from 0 to 63, each once within a row
- counts: int32 [32, 3], P(('gx', 'gy', 'gz')), may hold values from 0 to 32, as said below
Outputs:
- gas_out: float32 [6, 32, 32, 256], P(None, 'gx', 'gy', 'gz')
- moved_parcels: float32 [2048, 5, 128], P(('gx', 'gy', 'gz'))
Inputs may be any that keep to these rules, and one draw needn't show every extreme that they name: `gas`: gas density lies in 0.8 to 1.6, pressure in 0.8 to 1.6, velocities within 0.8, vapour fraction in 0.05 to 0.3. `parcels`: parcel masses lie in 0.2 to 2, temperatures in 0.3 to 1.2, velocities in -1 to 1.5. `counts`: kept is at most 32, forward and back each at most 16; each bound is reached in every draw.
All inputs are finite; a program needn't handle non-finite values.
Results may differ from a plain program's by a relative error of at most 0.00002.
Values sent between devices are 32-bit elements; how exact they have to be, the bound alone decides.
A program may use at most 64 MiB of HBM per device.

v0:
```python
import functools

import jax
import jax.numpy as jnp
from jax import lax
from jax.experimental import pallas as pl
from jax.experimental.pallas import tpu as pltpu
from jax.sharding import PartitionSpec as P

GAMMA = 1.4
TIME_STEP = 0.1
RATE = 3.0
ACTIVATION = 2.0
HEAT = 5.0
DRAG_RELAX_TIME = 0.4
HEATING_RELAX = 0.6
EVAP_RATE = 1.5
LIQUID_HEAT = 2.0
AXES = ("gx", "gy", "gz")
MESH = pl.DeviceIdType.MESH
F32 = jnp.float32
BF16 = jnp.bfloat16


def pressure_of(u):
    motion_energy = u[1] * u[1] + u[2] * u[2] + u[3] * u[3]
    return (GAMMA - 1.0) * (u[4] - 0.5 * motion_energy / u[0])


def base_of(u):
    inv = 1.0 / u[0]
    pressure = (GAMMA - 1.0) * (u[4] - 0.5 * inv * (u[1] * u[1] + u[2] * u[2] + u[3] * u[3]))
    return inv, pressure, jnp.sqrt(GAMMA * pressure * inv)


def directional(u, base, k):
    inv, pressure, sound = base
    along = u[1 + k] * inv
    flux = [u[1 + k], u[1] * along, u[2] * along, u[3] * along, (u[4] + pressure) * along, u[5] * along]
    flux[1 + k] = flux[1 + k] + pressure
    return flux, jnp.abs(along) + sound


def face(a, b):
    (ua, fa, sa), (ub, fb, sb) = a, b
    top = jnp.maximum(sa, sb)
    return [0.5 * ((fa[c] + fb[c]) - top * (ub[c] - ua[c])) for c in range(6)]


def pack_faces(ref, faces):
    planes, rows, lanes = ref.shape[1:]
    plane_id = lax.broadcasted_iota(jnp.int32, (planes, rows, lanes), 0)
    lane_id = lax.broadcasted_iota(jnp.int32, (planes, rows, lanes), 2)
    here = plane_id == lane_id
    for c in range(6):
        faces[0, 0, c] = ref[c, 0]
        faces[0, 1, c] = ref[c, planes - 1]
        faces[1, 0, c] = ref[c, :, 0, :]
        faces[1, 1, c] = ref[c, :, rows - 1, :]
        whole = ref[c]
        for side, lane in ((0, 0), (1, lanes - 1)):
            column = jnp.broadcast_to(whole[:, :, lane : lane + 1], (planes, rows, lanes))
            column = jnp.where(here | ((plane_id == 0) & (lane_id >= planes)), column, 0.0)
            faces[2, side, c] = jnp.sum(column, axis=0)


def inner_change(ref, change):
    planes, rows, lanes = ref.shape[1:]
    place_ids = [lax.broadcasted_iota(jnp.int32, (rows, lanes), d) for d in range(2)]
    before, behind = None, None
    for x in range(planes):
        u = [ref[c, x] for c in range(6)]
        base = base_of(u)
        now = (u,) + directional(u, base, 0)
        burned = RATE * u[5] * jnp.exp(-ACTIVATION * u[0] / base[1])
        result = [None] * 4 + [HEAT * burned, -burned]
        for k in (1, 2):
            flux, speed = directional(u, base, k)
            length = (rows, lanes)[k - 1]
            ahead = lambda v: pltpu.roll(v, length - 1, k - 1)
            upper = face((u, flux, speed), ([ahead(v) for v in u], [ahead(v) for v in flux], ahead(speed)))
            for c in range(6):
                h = jnp.where(place_ids[k - 1] == length - 1, 0.0, upper[c])
                d = pltpu.roll(h, 1, k - 1) - h
                result[c] = d if result[c] is None else result[c] + d
        if x > 0:
            between = face(before, now)
            for c in range(6):
                change[c, x - 1] = behind[c] - between[c]
                result[c] = result[c] + between[c]
        before, behind = now, result
    for c in range(6):
        change[c, planes - 1] = behind[c]


def edge_states(faces, states):
    for k in range(3):
        for side in range(2):
            u = [faces[k, side, c] for c in range(6)]
            flux, speed = directional(u, base_of(u), k)
            for c in range(6):
                states[k, side, c] = flux[c]
            states[k, side, 6] = speed


def full_change(change, faces, states, ghosts):
    shape = change.shape[1:]
    planes, rows, lanes = shape
    row_id = lax.broadcasted_iota(jnp.int32, shape, 1)
    lane_id = lax.broadcasted_iota(jnp.int32, shape, 2)
    edges = []
    for k in range(3):
        own, out = [], []
        for side in range(2):
            u = [ghosts[k, side, c] for c in range(6)]
            out.append((u,) + directional(u, base_of(u), k))
            own.append(([faces[k, side, c] for c in range(6)], [states[k, side, c] for c in range(6)], states[k, side, 6]))
        edges.append((face(out[0], own[0]), face(own[1], out[1])))
    result = []
    for c in range(6):
        low, high = edges[1][0][c], edges[1][1][c]
        low, high = [jnp.broadcast_to(v[:, None, :], shape) for v in (low, high)]
        total = change[c] + jnp.where(row_id == 0, low, jnp.where(row_id == rows - 1, -high, 0.0))
        low, high = edges[2][0][c], edges[2][1][c]
        low, high = [
            jnp.stack([jnp.broadcast_to(v[:, x : x + 1], (rows, lanes)) for x in range(planes)]) for v in (low, high)
        ]
        total = total + jnp.where(lane_id == 0, low, jnp.where(lane_id == lanes - 1, -high, 0.0))
        low, high = edges[0][0][c], edges[0][1][c]
        first, last = total[:1] + low[None], total[-1:] - high[None]
        result.append(jnp.concatenate([first, total[1:-1], last], axis=0))
    return result


def parcel_update(drop, gas):
    inv = 1.0 / gas[0]
    gas_velocity = [gas[1] * inv, gas[2] * inv, gas[3] * inv]
    gas_temp = pressure_of(gas) * inv
    vapour = gas[5] * inv
    mass, temp = drop[3], drop[4]
    root = jnp.sqrt(mass)
    inv_root = 1.0 / root
    new_mass = mass * jnp.exp(-TIME_STEP * EVAP_RATE * gas_temp * inv_root / (1.0 + vapour * vapour))
    drag = jnp.exp((-TIME_STEP / DRAG_RELAX_TIME) * inv_root)
    warm = jnp.exp((-TIME_STEP / HEATING_RELAX) * inv_root)
    new_velocity = [gas_velocity[d] + (drop[d] - gas_velocity[d]) * drag for d in range(3)]
    new_temp = gas_temp + (temp - gas_temp) * warm
    lost = mass - new_mass
    momentum = [mass * drop[d] - new_mass * new_velocity[d] for d in range(3)]
    before = drop[0] * drop[0] + drop[1] * drop[1] + drop[2] * drop[2]
    after = new_velocity[0] * new_velocity[0] + new_velocity[1] * new_velocity[1] + new_velocity[2] * new_velocity[2]
    energy = 0.5 * (mass * before - new_mass * after) + LIQUID_HEAT * (mass * temp - new_mass * new_temp)
    return new_velocity + [new_mass, new_temp], [lost] + momentum + [energy]


def split_three(v):
    head = v.astype(BF16)
    rest = v - head.astype(F32)
    middle = rest.astype(BF16)
    return head, middle, (rest - middle.astype(F32)).astype(BF16)


def kernel(
    sizes, counts_h, order_h, gas_h, parcels_h, cells_h,
    gas_out, moved,
    counts_v, order_v, gas, parcels, cells, fetch,
    faces, ghosts, states, change, stepped, copies, hot, high_hot, sources, live, spread,
    choice, blocks, own_blocks, going, coming, arrived, count_out, count_in,
    face_send, face_recv, move_send, move_recv, count_send, count_recv,
):
    place = [lax.axis_index(a) for a in AXES]
    planes, rows, lanes = gas.shape[1:]
    slots = parcels.shape[1]
    cap = slots // 4
    group = 8
    chunks = slots // group
    half = planes // 2
    wide = half * rows

    inputs = ((gas_h, gas), (counts_h, counts_v), (order_h, order_v), (cells_h, cells), (parcels_h, parcels))
    fetches = [pltpu.make_async_copy(src, dst, fetch.at[i]) for i, (src, dst) in enumerate(inputs)]
    for copy in fetches:
        copy.start()

    def has(k, side):
        return place[k] > 0 if side == 0 else place[k] < sizes[k] - 1

    def neighbour(k, side):
        return {AXES[k]: lax.rem(place[k] + (sizes[k] - 1 if side == 0 else 1), sizes[k])}

    def copy_to(k, side, src, dst, send, recv):
        return pltpu.make_async_remote_copy(
            src_ref=src, dst_ref=dst, send_sem=send, recv_sem=recv,
            device_id=neighbour(k, side), device_id_type=MESH,
        )

    def face_copy(turn, k, side):
        return copy_to(
            k, side, faces.at[turn, k, side], ghosts.at[turn, k, 1 - side],
            face_send.at[turn, k, side], face_recv.at[turn, k, 1 - side],
        )

    def count_copy(side):
        return copy_to(0, side, count_out.at[side], count_in.at[1 - side], count_send.at[side], count_recv.at[1 - side])

    def move_copy(side):
        return copy_to(0, side, going.at[side], coming.at[1 - side], move_send.at[side], move_recv.at[1 - side])

    links = [(k, side) for k in range(3) for side in range(2) if sizes[k] > 1]

    barrier = pltpu.get_barrier_semaphore()
    arrivals = 0
    for k, side in links:
        @pl.when(has(k, side))
        def _():
            pl.semaphore_signal(barrier, inc=1, device_id=neighbour(k, side), device_id_type=MESH)
        arrivals = arrivals + has(k, side).astype(jnp.int32)

    for copy in fetches[:4]:
        copy.wait()
    kept, forward, backward = [counts_v[0:1, i : i + 1] for i in range(3)]
    pack_faces(gas, faces.at[0])
    count_out[0] = jnp.broadcast_to(backward, count_out.shape[1:])
    count_out[1] = jnp.broadcast_to(forward, count_out.shape[1:])
    for side in range(2):
        @pl.when(jnp.logical_not(has(0, side)))
        def _():
            count_in[side] = jnp.zeros(count_in.shape[1:], jnp.int32)
            coming[side] = jnp.zeros(coming.shape[1:], F32)

    pl.semaphore_wait(barrier, arrivals)

    def send_faces(turn):
        for k in range(3):
            for side in range(2):
                if (k, side) in links:
                    @pl.when(has(k, side))
                    def _():
                        face_copy(turn, k, side).start()

                @pl.when(jnp.logical_not(has(k, side)))
                def _():
                    ghosts[turn, k, side] = faces[turn, k, side]

    def receive_faces(turn):
        for k, side in links:
            @pl.when(has(k, side))
            def _():
                face_copy(turn, k, 1 - side).wait_recv()

    send_faces(0)
    for side in range(2):
        if sizes[0] > 1:
            @pl.when(has(0, side))
            def _():
                count_copy(side).start()

    def build(i, carry):
        cell = cells[pl.ds(i * group, group), :]
        column = (cell % lanes) + (cell // (lanes * wide)) * lanes
        high = (cell // lanes) % wide
        column = column.astype(F32).T
        column_id = lax.broadcasted_iota(jnp.int32, (lanes, 2 * lanes), 1).astype(F32)
        row_id = lax.broadcasted_iota(jnp.int32, (wide, lanes), 0)
        for j in range(group):
            here = slice(j * lanes, (j + 1) * lanes)
            match = jnp.broadcast_to(column[:, j : j + 1], column_id.shape) == column_id
            hot[pl.ds(pl.multiple_of((i * group + j) * lanes, lanes), lanes), :] = jnp.where(match, 1.0, 0.0).astype(BF16)
            high_hot[i, :, here] = jnp.where(row_id == high[j : j + 1, :], 1.0, 0.0).astype(BF16)
        return carry

    inner_change(gas, change)
    edge_states(faces.at[0], states)
    lax.fori_loop(0, chunks // 2, build, 0)
    receive_faces(0)
    both = full_change(change, faces.at[0], states, ghosts.at[0])
    for c in range(6):
        stepped[c] = gas[c] + TIME_STEP * both[c]
    pack_faces(stepped, faces.at[1])
    send_faces(1)
    inner_change(stepped, change)
    edge_states(faces.at[1], states)

    lax.fori_loop(chunks // 2, chunks, build, 0)
    fetches[4].wait()
    slot_id = lax.broadcasted_iota(jnp.int32, (slots, slots), 0)
    turn_id = lax.broadcasted_iota(jnp.int32, (slots, slots), 1)
    used = (order_v[...] == slot_id) & (turn_id < kept + forward + backward)
    used = jnp.sum(jnp.where(used, 1.0, 0.0), axis=1, keepdims=True)
    live[...] = jnp.broadcast_to(used, live.shape)

    rows_out = slots + 2 * cap
    take_id = lax.broadcasted_iota(jnp.int32, (rows_out, slots), 0)
    from_id = lax.broadcasted_iota(jnp.int32, (rows_out, slots), 1)
    spot = jnp.where(take_id < slots, take_id, take_id - slots + kept)
    spot = jnp.where(take_id < slots + cap, spot, take_id - slots - cap + kept + forward)
    origin = jnp.where(from_id == spot, order_v[...].astype(F32), 0.0)
    origin = jnp.sum(origin, axis=1, keepdims=True)
    wide_id = lax.broadcasted_iota(jnp.int32, choice.shape, 1) % slots
    take_id = lax.broadcasted_iota(jnp.int32, choice.shape, 0)
    chosen = (wide_id.astype(F32) == origin) & ((take_id < kept) | (take_id >= slots))
    choice[...] = jnp.where(chosen, 1.0, 0.0).astype(BF16)

    receive_faces(1)
    both = full_change(change, faces.at[1], states, ghosts.at[1])
    for c in range(6):
        v = 0.5 * gas[c] + 0.5 * (stepped[c] + TIME_STEP * both[c])
        stepped[c] = v
        for x in range(planes):
            for y in range(rows):
                copies[x, y, c] = jnp.broadcast_to(v[x, y : y + 1, :], (group, lanes))

    def spread_out(i):
        source = [sources[i, c] for c in range(5)]
        head = [v.astype(BF16).astype(F32) for v in source]
        rest = [v - h for v, h in zip(source, head)]
        for j in range(group):
            here = pl.ds(pl.multiple_of((i * group + j) * lanes, lanes), lanes)
            match = high_hot[i, :, j * lanes : (j + 1) * lanes]
            for c, v in enumerate(head + rest):
                term = jnp.broadcast_to(v[j : j + 1, :], (wide, lanes)).astype(BF16)
                spread[c * wide : (c + 1) * wide, here] = match * term

    for c in range(5):
        sources[0, c] = jnp.zeros((group, lanes), F32)

    def gather(i, carry):
        spread_out(jnp.maximum(i - 1, 0))
        block = pl.ds(i * group, group)
        cell = cells[block, :]
        lane, high = cell % lanes, cell // lanes
        got = [jnp.zeros((group, lanes), F32)] * 6
        for x in range(planes):
            for y in range(rows):
                match = high == x * rows + y
                for c in range(6):
                    value = jnp.take_along_axis(copies[x, y, c], lane, axis=1, mode="promise_in_bounds")
                    got[c] = jnp.where(match, value, got[c])
        new, source = parcel_update([parcels[d, block, :] for d in range(5)], got)
        for d in range(5):
            for part, term in enumerate(split_three(new[d])):
                blocks[d, pl.ds(part * slots + i * group, group), :] = term.astype(F32)
        for c in range(5):
            sources[i, c] = source[c] * live[block, :]
        return carry

    lax.fori_loop(0, chunks, gather, 0)

    for d in range(5):
        sorted_blocks = jnp.dot(choice[...], blocks[d].astype(BF16), preferred_element_type=F32)
        own_blocks[d] = sorted_blocks[:slots]
        going[1, d] = sorted_blocks[slots : slots + cap]
        going[0, d] = sorted_blocks[slots + cap :]
    for side in range(2):
        if sizes[0] > 1:
            @pl.when(has(0, side))
            def _():
                move_copy(side).start()

    spread_out(chunks - 1)
    total = jnp.dot(spread[...], hot[...], preferred_element_type=F32)
    for c in range(6):
        s = 0 if c == 5 else c
        summed = total[s * wide : (s + 1) * wide, :] + total[(5 + s) * wide : (6 + s) * wide, :]
        for part in range(2):
            part_sum = summed[:, part * lanes : (part + 1) * lanes].reshape(half, rows, lanes)
            here = slice(part * half, (part + 1) * half)
            gas_out[c, here] = stepped[c, here] + part_sum

    for side in range(2):
        if sizes[0] > 1:
            @pl.when(has(0, side))
            def _():
                count_copy(1 - side).wait_recv()
                move_copy(1 - side).wait_recv()

    place_shape = (slots, 6 * cap)
    slot_id = lax.broadcasted_iota(jnp.int32, place_shape, 0)
    block_id = lax.broadcasted_iota(jnp.int32, place_shape, 1) % (2 * cap)
    lower = jnp.broadcast_to(count_in[0, 0:1, : 6 * cap], place_shape)
    upper = jnp.broadcast_to(count_in[1, 0:1, : 6 * cap], place_shape)
    from_lower = (slot_id - kept == block_id) & (block_id < cap) & (block_id < lower)
    above = block_id - cap
    from_upper = (slot_id - kept - lower == above) & (above >= 0) & (above < upper)
    fill = jnp.where(from_lower | from_upper, 1.0, 0.0).astype(BF16)
    for d in range(5):
        for side in range(2):
            for part, term in enumerate(split_three(coming[side, d])):
                start = part * 2 * cap + side * cap
                arrived[d, start : start + cap, :] = term
        moved[d] = own_blocks[d] + jnp.dot(fill, arrived[d], preferred_element_type=F32)

    for turn in range(2):
        for k, side in links:
            @pl.when(has(k, side))
            def _():
                face_copy(turn, k, side).wait_send()
    for side in range(2):
        if sizes[0] > 1:
            @pl.when(has(0, side))
            def _():
                count_copy(side).wait_send()
                move_copy(side).wait_send()


def body(sizes, gas, parcels, home_cell_index, order, counts):
    planes, rows, lanes = gas.shape[1:]
    parcels = jnp.transpose(parcels, (1, 0, 2))
    slots = parcels.shape[1]
    group = 8
    chunks = slots // group
    wide = planes // 2 * rows
    cap = slots // 4
    vmem = pl.BlockSpec(memory_space=pltpu.VMEM)
    hbm = pl.BlockSpec(memory_space=pltpu.HBM)
    dma = pltpu.SemaphoreType.DMA
    gas_out, moved = pl.pallas_call(
        functools.partial(kernel, sizes),
        out_shape=(pltpu.VMEM(gas.shape, F32), pltpu.VMEM(parcels.shape, F32)),
        in_specs=[hbm] * 5,
        out_specs=(vmem, vmem),
        scratch_shapes=[
            pltpu.VMEM(counts.shape, jnp.int32),
            pltpu.VMEM(order.shape, jnp.int32),
            pltpu.VMEM(gas.shape, F32),
            pltpu.VMEM(parcels.shape, F32),
            pltpu.VMEM(home_cell_index.shape, jnp.int32),
            dma((5,)),
            pltpu.VMEM((2, 3, 2, 6, rows, lanes), F32),
            pltpu.VMEM((2, 3, 2, 6, rows, lanes), F32),
            pltpu.VMEM((3, 2, 7, rows, lanes), F32),
            pltpu.VMEM(gas.shape, F32),
            pltpu.VMEM(gas.shape, F32),
            pltpu.VMEM((planes, rows, 6, group, lanes), F32),
            pltpu.VMEM((slots * lanes, 2 * lanes), BF16),
            pltpu.VMEM((chunks, wide, group * lanes), BF16),
            pltpu.VMEM((chunks, 5, group, lanes), F32),
            pltpu.VMEM((slots, lanes), F32),
            pltpu.VMEM((10 * wide, slots * lanes), BF16),
            pltpu.VMEM((slots + 2 * cap, 3 * slots), BF16),
            pltpu.VMEM((5, 3 * slots, lanes), F32),
            pltpu.VMEM(parcels.shape, F32),
            pltpu.VMEM((2, 5, cap, lanes), F32),
            pltpu.VMEM((2, 5, cap, lanes), F32),
            pltpu.VMEM((5, 6 * cap, lanes), BF16),
            pltpu.VMEM((2, 8, lanes), jnp.int32),
            pltpu.VMEM((2, 8, lanes), jnp.int32),
            dma((2, 3, 2)), dma((2, 3, 2)), dma((2,)), dma((2,)), dma((2,)), dma((2,)),
        ],
        compiler_params=pltpu.CompilerParams(
            collective_id=0, has_side_effects=True, vmem_limit_bytes=48 * 1024 * 1024
        ),
    )(*[pltpu.with_memory_space_constraint(v, pltpu.HBM) for v in (counts, order, gas, parcels, home_cell_index)])
    return gas_out, jnp.transpose(moved, (1, 0, 2))


def solution(mesh):
    in_specs = (
        P(None, "gx", "gy", "gz"),
        P(("gx", "gy", "gz"), None, None),
        P(("gx", "gy", "gz"), None),
        P(("gx", "gy", "gz"), None),
        P(("gx", "gy", "gz"), None),
    )
    out_specs = (P(None, "gx", "gy", "gz"), P(("gx", "gy", "gz"), None, None))
    sizes = tuple(mesh.shape[a] for a in AXES)
    return jax.shard_map(
        functools.partial(body, sizes), mesh=mesh, in_specs=in_specs, out_specs=out_specs, check_vma=False
    )
```

profile of v0, /device:TPU:0, one launch (start us, length us, event | category | flops | bytes accessed | tf_op | source)
XLA Modules:
  0.0 21.6 jit_solution(6889449221881186381)
XLA Ops:
  0.6 19.6 %shard_map.68 = (f32[6,8,8,128]{3,2,1,0:T(8,128)S(1)}, f32[5,64,128]{2,1,0:T(8,128)S(1)}) custom-call(s32[1,3]{1,0:T(1,128)} %counts_h.1, s32[1,64]{1,0:T(1,128)} %order_h.1, f32[6,8,8,128]{3,2,1,0:T(8,128)} %gas_h.1, f32[5,64,128]{2,1,0:T(8,128)} %bitcast.3, s32[64,128]{1,0:T(8,128)} %cells_h.1), custom_call_target="tpu_custom_call" | custom-call | tf_op jit(solution)/shard_map/pallas_call | solution.py:417
  20.2 0.7 %copy.9 = f32[6,8,8,128]{3,2,1,0:T(8,128)} copy(f32[6,8,8,128]{3,2,1,0:T(8,128)S(1)} %get-tuple-element.6) | data formatting | bytes 393216
  20.9 0.7 %copy.10 = f32[64,5,128]{2,0,1:T(8,128)} copy(f32[64,5,128]{2,0,1:T(8,128)S(1)} %bitcast.2) | data formatting | bytes 327680
where the time goes:
time: 21.7 us; the launch traced here: 21.6 us
  Pallas kernels  19.6 us (90%)
  local copies, waits for them, and re-layouts  1.35 us (6%)
  between operations  0.64 us (3%)
    pallas_call x1, Pallas kernels, body(): pl.pallas_call(functools.partial(kernel, sizes), out_shape=(pltpu.VMEM(ga...  19.6 us
    unnamed x2, local copies, waits for them, and re-layouts  1.35 us

commit v1 on v0

--- a/solution.py
+++ b/solution.py
@@ -164,7 +164,7 @@
     sizes, counts_h, order_h, gas_h, parcels_h, cells_h,
     gas_out, moved,
     counts_v, order_v, gas, parcels, cells, fetch,
-    faces, ghosts, states, change, stepped, copies, hot, high_hot, sources, live, spread,
+    faces, ghosts, states, change, stepped, table, carried, hot, high_hot, sources, live, spread,
     choice, blocks, own_blocks, going, coming, arrived, count_out, count_in,
     face_send, face_recv, move_send, move_recv, count_send, count_recv,
 ):
@@ -257,16 +257,17 @@
 
     def build(i, carry):
         cell = cells[pl.ds(i * group, group), :]
-        column = (cell % lanes) + (cell // (lanes * wide)) * lanes
-        high = (cell // lanes) % wide
-        column = column.astype(F32).T
-        column_id = lax.broadcasted_iota(jnp.int32, (lanes, 2 * lanes), 1).astype(F32)
-        row_id = lax.broadcasted_iota(jnp.int32, (wide, lanes), 0)
+        column = ((cell % lanes) + (cell // (lanes * wide)) * lanes).astype(F32)
+        high = ((cell // lanes) % wide).astype(F32)
+        column_id = lax.broadcasted_iota(jnp.int32, (2 * lanes, lanes), 0).astype(F32).astype(BF16)
+        row_id = lax.broadcasted_iota(jnp.int32, (wide, lanes), 0).astype(F32).astype(BF16)
+        one, none = jnp.ones((), BF16), jnp.zeros((), BF16)
         for j in range(group):
-            here = slice(j * lanes, (j + 1) * lanes)
-            match = jnp.broadcast_to(column[:, j : j + 1], column_id.shape) == column_id
-            hot[pl.ds(pl.multiple_of((i * group + j) * lanes, lanes), lanes), :] = jnp.where(match, 1.0, 0.0).astype(BF16)
-            high_hot[i, :, here] = jnp.where(row_id == high[j : j + 1, :], 1.0, 0.0).astype(BF16)
+            here = pl.ds(pl.multiple_of((i * group + j) * lanes, lanes), lanes)
+            match = jnp.broadcast_to(column[j : j + 1, :], column_id.shape).astype(BF16) == column_id
+            hot[:, here] = jnp.where(match, one, none)
+            match = jnp.broadcast_to(high[j : j + 1, :], row_id.shape).astype(BF16) == row_id
+            high_hot[:, here] = jnp.where(match, one, none)
         return carry
 
     inner_change(gas, change)
@@ -306,45 +307,51 @@
     for c in range(6):
         v = 0.5 * gas[c] + 0.5 * (stepped[c] + TIME_STEP * both[c])
         stepped[c] = v
-        for x in range(planes):
-            for y in range(rows):
-                copies[x, y, c] = jnp.broadcast_to(v[x, y : y + 1, :], (group, lanes))
-
-    def spread_out(i):
+        for part in range(2):
+            terms = split_three(v[part * half : (part + 1) * half].reshape(wide, lanes))
+            for t in range(2):
+                start = (6 * t + c) * wide
+                table[start : start + wide, part * lanes : (part + 1) * lanes] = terms[t]
+
+    def spread_out(i, carry):
         source = [sources[i, c] for c in range(5)]
         head = [v.astype(BF16).astype(F32) for v in source]
         rest = [v - h for v, h in zip(source, head)]
         for j in range(group):
             here = pl.ds(pl.multiple_of((i * group + j) * lanes, lanes), lanes)
-            match = high_hot[i, :, j * lanes : (j + 1) * lanes]
+            match = high_hot[:, here]
             for c, v in enumerate(head + rest):
                 term = jnp.broadcast_to(v[j : j + 1, :], (wide, lanes)).astype(BF16)
                 spread[c * wide : (c + 1) * wide, here] = match * term
-
-    for c in range(5):
-        sources[0, c] = jnp.zeros((group, lanes), F32)
+        return carry
 
     def gather(i, carry):
-        spread_out(jnp.maximum(i - 1, 0))
-        block = pl.ds(i * group, group)
+        for n in range(2):
+            gather_chunk(2 * i + n)
+        return carry
+
+    def gather_chunk(i):
+        block = pl.ds(pl.multiple_of(i * group, group), group)
         cell = cells[block, :]
-        lane, high = cell % lanes, cell // lanes
-        got = [jnp.zeros((group, lanes), F32)] * 6
-        for x in range(planes):
-            for y in range(rows):
-                match = high == x * rows + y
-                for c in range(6):
-                    value = jnp.take_along_axis(copies[x, y, c], lane, axis=1, mode="promise_in_bounds")
-                    got[c] = jnp.where(match, value, got[c])
+        high = (cell // lanes) % wide
+        row_id = lax.broadcasted_iota(jnp.int32, (wide, lanes), 0)
+        every = pl.ds(pl.multiple_of(i * group * lanes, group * lanes), group * lanes)
+        found = jnp.dot(table[...], hot[:, every], preferred_element_type=F32)
+        for j in range(group):
+            here = slice(j * lanes, (j + 1) * lanes)
+            match = row_id == high[j : j + 1, :]
+            for c in range(6):
+                v = found[c * wide : (c + 1) * wide, here] + found[(6 + c) * wide : (7 + c) * wide, here]
+                carried[i, c, j : j + 1, :] = jnp.sum(jnp.where(match, v, 0.0), axis=0, keepdims=True)
+        got = [carried[i, c] for c in range(6)]
         new, source = parcel_update([parcels[d, block, :] for d in range(5)], got)
         for d in range(5):
             for part, term in enumerate(split_three(new[d])):
-                blocks[d, pl.ds(part * slots + i * group, group), :] = term.astype(F32)
+                blocks[d, pl.ds(pl.multiple_of(part * slots + i * group, group), group), :] = term.astype(F32)
         for c in range(5):
             sources[i, c] = source[c] * live[block, :]
-        return carry
-
-    lax.fori_loop(0, chunks, gather, 0)
+
+    lax.fori_loop(0, chunks // 2, gather, 0)
 
     for d in range(5):
         sorted_blocks = jnp.dot(choice[...], blocks[d].astype(BF16), preferred_element_type=F32)
@@ -357,8 +364,8 @@
             def _():
                 move_copy(side).start()
 
-    spread_out(chunks - 1)
-    total = jnp.dot(spread[...], hot[...], preferred_element_type=F32)
+    lax.fori_loop(0, chunks, spread_out, 0)
+    total = lax.dot_general(spread[...], hot[...], (((1,), (1,)), ((), ())), preferred_element_type=F32)
     for c in range(6):
         s = 0 if c == 5 else c
         summed = total[s * wide : (s + 1) * wide, :] + total[(5 + s) * wide : (6 + s) * wide, :]
@@ -431,9 +438,10 @@
             pltpu.VMEM((3, 2, 7, rows, lanes), F32),
             pltpu.VMEM(gas.shape, F32),
             pltpu.VMEM(gas.shape, F32),
-            pltpu.VMEM((planes, rows, 6, group, lanes), F32),
-            pltpu.VMEM((slots * lanes, 2 * lanes), BF16),
-            pltpu.VMEM((chunks, wide, group * lanes), BF16),
+            pltpu.VMEM((12 * wide, 2 * lanes), BF16),
+            pltpu.VMEM((chunks, 6, group, lanes), F32),
+            pltpu.VMEM((2 * lanes, slots * lanes), BF16),
+            pltpu.VMEM((wide, slots * lanes), BF16),
             pltpu.VMEM((chunks, 5, group, lanes), F32),
             pltpu.VMEM((slots, lanes), F32),
             pltpu.VMEM((10 * wide, slots * lanes), BF16),

time: 21.7 us -> 19.5 us (0.90)
  Pallas kernels: 19.6 us -> 17.4 us
    pallas_call x1, Pallas kernels: 19.6 us -> 17.4 us  [body(): pl.pallas_call(functools.partial(kernel, sizes), out_shape=(pltpu.VMEM(ga...]
where the time goes in v1:
time: 19.5 us; the launch traced here: 19.4 us
  Pallas kernels  17.4 us (89%)
  local copies, waits for them, and re-layouts  1.35 us (7%)
  between operations  0.64 us (3%)
    pallas_call x1, Pallas kernels, body(): pl.pallas_call(functools.partial(kernel, sizes), out_shape=(pltpu.VMEM(ga...  17.4 us
    unnamed x2, local copies, waits for them, and re-layouts  1.35 us

profile of v1, /device:TPU:0, one launch (start us, length us, event | category | flops | bytes accessed | tf_op | source)
XLA Modules:
  0.0 19.4 jit_solution(14688858866521033826)
XLA Ops:
  0.6 17.4 %shard_map.68 = (f32[6,8,8,128]{3,2,1,0:T(8,128)S(1)}, f32[5,64,128]{2,1,0:T(8,128)S(1)}) custom-call(s32[1,3]{1,0:T(1,128)} %counts_h.1, s32[1,64]{1,0:T(1,128)} %order_h.1, f32[6,8,8,128]{3,2,1,0:T(8,128)} %gas_h.1, f32[5,64,128]{2,1,0:T(8,128)} %bitcast.3, s32[64,128]{1,0:T(8,128)} %cells_h.1), custom_call_target="tpu_custom_call" | custom-call | tf_op jit(solution)/shard_map/pallas_call | solution.py:424
  18.0 0.7 %copy.9 = f32[6,8,8,128]{3,2,1,0:T(8,128)} copy(f32[6,8,8,128]{3,2,1,0:T(8,128)S(1)} %get-tuple-element.6) | data formatting | bytes 393216
  18.7 0.7 %copy.10 = f32[64,5,128]{2,0,1:T(8,128)} copy(f32[64,5,128]{2,0,1:T(8,128)S(1)} %bitcast.2) | data formatting | bytes 327680
